TPU v7x, 1024 devices: a whole 4x4x32 slice. The times are simulated.
1024 devices in a mesh: ep: 16 (over x, y), tp: 64 (over z, core).
Axes of the slice: x: 4, y: 4, z: 32, core: 2. Of those that a mesh axis runs over, the one named last changes fastest.
Arguments:
- grad_out: bfloat16 [16384, 3584], P('tp', 'ep'), may hold values from -6 to 6
- route_probs: float32 [16384, 2], P('tp'), may hold values from 0.2 to 1
- routes: int32 [16384, 2], P('tp'), may hold values from 0 to 63, all different within a row; in each aligned block of 256 rows (0 to 255, 256 to 511, ...) at most 12 rows name the same one
- saved_up: bfloat16 [64, 2432, 768], P('tp', 'ep'), may hold values from -6 to 6
- w_up: bfloat16 [64, 3584, 2432], P('tp', 'ep'), may hold values from -0.09375 to 0.09375
- w_down: bfloat16 [64, 2432, 3584], P('tp', None, 'ep'), may hold values from -0.125 to 0.125
Outputs:
- input_grad: bfloat16 [16384, 3584], P('tp', 'ep')
Inputs may be any that keep to these rules, and one draw needn't show every extreme that they name: `routes`: the two experts of a row differ. In each aligned block of 256 rows no expert is named by more than 12 rows, a bound that some block reaches.
All inputs are finite; a program needn't handle non-finite values.
Results may differ from a plain program's by a relative error of at most 0.023.
Values may be sent and summed in bfloat16 or wider, within the bound.
A program may use at most 32 MiB of HBM per device.

v0:
```python
import jax
import jax.numpy as jnp
from jax import lax
from jax.sharding import PartitionSpec as P


def on_device(grad_out, route_probs, routes, saved_up, w_up, w_down):
    tok_count, width_local = grad_out.shape
    expert_count = lax.axis_size("tp")
    slot_count = saved_up.shape[2]
    capacity = slot_count // expert_count
    flat_routes = routes.reshape(-1)
    experts_iota = jnp.arange(expert_count, dtype=jnp.int32)
    onehot = (flat_routes[:, None] == experts_iota[None, :]).astype(jnp.int32)
    before = jnp.cumsum(onehot, axis=0) - onehot
    earlier = jnp.sum(before * onehot, axis=1)
    slot_index = flat_routes * capacity + earlier
    pair_rows = jnp.repeat(grad_out, 2, axis=0)
    outgoing = (
        jnp.zeros((expert_count * capacity, width_local), jnp.bfloat16)
        .at[slot_index]
        .set(pair_rows)
    )
    outgoing = outgoing.reshape(expert_count, capacity, width_local)
    received = lax.all_to_all(outgoing, "tp", split_axis=0, concat_axis=0, tiled=True).reshape(
        slot_count, width_local
    )
    down_local = w_down[0]
    up_local = w_up[0]
    saved = saved_up[0].astype(jnp.float32)
    hidden_local = saved.shape[0]
    weight_block = lax.all_to_all(down_local, "ep", split_axis=0, concat_axis=1, tiled=True)
    segment = lax.all_gather(received, "ep", axis=1, tiled=True)
    seg_width = segment.shape[1]
    blocks = seg_width // width_local
    weights = weight_block
    partials = jnp.einsum(
        "fbd,sbd->bfs",
        weights.reshape(hidden_local, blocks, width_local),
        segment.reshape(slot_count, blocks, width_local),
        preferred_element_type=jnp.float32,
    )
    rounded = lax.optimization_barrier(partials.astype(jnp.bfloat16)).astype(jnp.float32)
    hidden_grad = jnp.sum(rounded, axis=0)
    gate_value = jax.nn.sigmoid(saved)
    grad_up = (hidden_grad * gate_value * (1.0 + saved * (1.0 - gate_value))).astype(jnp.bfloat16)
    weights = up_local
    expert_grad = jnp.dot(
        weights,
        lax.all_gather(grad_up, "ep", axis=0, tiled=True),
        preferred_element_type=jnp.float32,
    ).astype(jnp.bfloat16)
    returned_grad = lax.all_to_all(
        expert_grad.reshape(width_local, expert_count, capacity),
        "tp",
        split_axis=1,
        concat_axis=1,
        tiled=True,
    )
    flat_returned = returned_grad.reshape(width_local, expert_count * capacity)
    picked = jnp.take(flat_returned, slot_index, axis=1).astype(jnp.float32)
    weighted = picked.reshape(width_local, tok_count, 2) * route_probs[None, :, :]
    result = jnp.sum(weighted, axis=2).T
    return result.astype(jnp.bfloat16)


def solution(mesh):
    return jax.shard_map(
        on_device,
        mesh=mesh,
        in_specs=(
            P("tp", "ep"),
            P("tp", None),
            P("tp", None),
            P("tp", "ep", None),
            P("tp", "ep", None),
            P("tp", None, "ep"),
        ),
        out_specs=P("tp", "ep"),
        check_vma=False,
    )
```

profile of v0, /device:TPU:2, one launch (start us, length us, event | category | flops | bytes accessed | tf_op | source)
XLA Modules:
  0.0 381.0 jit_solution(5661192779035555805)
XLA Ops:
  6.5 0.0 copy-start
  6.5 0.0 all-gather.3.cloned.1.call-start
  6.5 1.0 copy.30
  7.5 0.1 eq.26
  7.7 0.1 reshape.89
  7.8 0.7 broadcast_multiply_fusion
  8.5 1.2 reduce-window.6
  9.7 0.2 slice_reduce_fusion
  10.0 0.1 copy.35
  10.1 0.1 mul.42
  10.3 1.0 copy.36
  11.3 0.1 broadcast_in_dim.21
  11.4 0.2 reshape.110
  11.7 0.1 fusion.13
  11.8 2.4 scatter_custom_fusion
  14.3 0.1 reshape.92
  14.4 94.9 %all_to_all.26 = bf16[64,12,224]{2,1,0:T(8,128)(2,1)S(1)} all-to-all(bf16[64,12,224]{2,1,0:T(8,128)(2,1)S(1)} %reshape.92), channel_id=1, replica_groups=mesh['ep'=16,'tp'=64] {'tp'}, dimensions={0} | all-to-all | bytes 688128 | tf_op jit(solution)/shard_map/all_to_all | solution.py:25
  109.3 0.2 reshape.93
  109.5 0.9 copy.37
  110.4 0.0 all-gather.3.cloned.1.call-update
  110.4 0.0 all-gather.5.cloned.1.call-start
  110.5 1.6 copy.38
  112.1 28.7 %all_to_all.27 = bf16[16,152,224]{2,1,0:T(8,128)(2,1)S(1)} all-to-all(bf16[16,152,224]{2,1,0:T(8,128)(2,1)} %bitcast.49), channel_id=1, replica_groups=mesh['ep'=16,'tp'=64] {'ep'}, dimensions={0} | all-to-all | bytes 2179072 | tf_op jit(solution)/shard_map/all_to_all | solution.py:32
  140.8 44.3 %all-gather.3.cloned.1.call-done = bf16[768,3584]{0,1:T(8,128)(2,1)} async-done(((bf16[768,224]{0,1:T(8,128)(2,1)}), bf16[768,3584]{0,1:T(8,128)(2,1)}) %all-gather.3.cloned.1.call-update) | async-done | bytes 5505040 | tf_op jit(solution)/shard_map/all_gather | solution.py:33
  185.1 3.7 convert_bitcast_fusion
  188.8 0.0 copy-start.2
  188.9 0.6 convert_reduce_fusion
  189.4 0.4 copy-done.2
  189.8 0.9 fusion.8
  190.7 0.0 all-gather.5.cloned.1.call-update
  190.7 0.0 copy-start.3
  190.7 0.0 copy-start.4
  190.7 85.4 %all-gather.5.cloned.1.call-done = bf16[2432,768]{1,0:T(8,128)(2,1)} async-done(((bf16[152,768]{1,0:T(8,128)(2,1)}), bf16[2432,768]{1,0:T(8,128)(2,1)}) %all-gather.5.cloned.1.call-update) | async-done | bytes 3735568 | tf_op jit(solution)/shard_map/all_gather | solution.py:50
  276.1 0.0 copy-done
  276.1 3.1 fusion.1
  279.2 0.2 copy.39
  279.4 0.9 reshape.95
  280.3 23.5 %all-to-all-start.2 = ((bf16[224,64,12]{0,2,1:T(8,128)(2,1)}), bf16[224,64,12]{0,2,1:T(8,128)(2,1)S(1)}, u32[]{:S(2)}, u32[]{:S(2)}) async-start(bf16[224,64,12]{0,2,1:T(8,128)(2,1)} %reshape.95), calls=%async_computation.2 | async-start | bytes 1048576 | tf_op jit(solution)/shard_map/all_to_all | solution.py:53
  303.8 0.1 reduce_sum.32
  304.0 0.1 copy.33
  304.1 0.2 copy.34
  304.3 0.1 copy.40
  304.4 65.2 %all-to-all-done.2 = bf16[224,64,12]{0,2,1:T(8,128)(2,1)S(1)} async-done(((bf16[224,64,12]{0,2,1:T(8,128)(2,1)}), bf16[224,64,12]{0,2,1:T(8,128)(2,1)S(1)}, u32[]{:S(2)}, u32[]{:S(2)}) %all-to-all-start.2) | async-done | bytes 344096 | tf_op jit(solution)/shard_map/all_to_all | solution.py:53
  369.6 0.2 reshape.96
  369.8 2.0 gather_fusion
  371.8 0.1 gather.7
  371.9 1.5 multiply_reduce_fusion
  373.4 0.8 copy.41
  (10 shorter events, 0.1 us)
Async XLA Ops:
  6.5 269.6 %copy-start = (bf16[1,224,2432]{2,1,0:T(8,128)(2,1)S(1)}, bf16[1,224,2432]{2,1,0:T(8,128)(2,1)}, u32[]{:S(2)}) copy-start(bf16[1,224,2432]{2,1,0:T(8,128)(2,1)} %param.10) | copy-start | bytes 3268612
  6.5 103.9 %copy-start.1 = (bf16[1,2432,224]{1,2,0:T(8,128)(2,1)S(1)}, bf16[1,2432,224]{1,2,0:T(8,128)(2,1)}, u32[]{:S(2)}) copy-start(bf16[1,2432,224]{1,2,0:T(8,128)(2,1)} %param.11) | copy-start | bytes 3268612
  6.5 178.6 %all-gather.3.cloned.1.call-start = ((), (), s32[]{:S(2)}) async-start(), calls=%async_computation.3 | async-start | bytes 5849088 | tf_op jit(solution)/shard_map/all_gather | solution.py:33
  110.4 165.7 %all-gather.5.cloned.1.call-start = ((), (), s32[]{:S(2)}) async-start(), calls=%async_computation.4 | async-start | bytes 3969024 | tf_op jit(solution)/shard_map/all_gather | solution.py:50
  188.8 0.9 copy-start.2
  190.7 113.4 %copy-start.3 = (s32[256,2]{0,1:T(2,128)S(1)}, s32[256,2]{0,1:T(2,128)}, u32[]{:S(2)}) copy-start(s32[256,2]{0,1:T(2,128)} %param.8) | copy-start | bytes 6148
  190.7 113.6 %copy-start.4 = (f32[256,2]{0,1:T(2,128)S(1)}, f32[256,2]{0,1:T(2,128)}, u32[]{:S(2)}) copy-start(f32[256,2]{0,1:T(2,128)} %param.7) | copy-start | bytes 6148
  280.3 89.3 %all-to-all-start.2 = ((bf16[224,64,12]{0,2,1:T(8,128)(2,1)}), bf16[224,64,12]{0,2,1:T(8,128)(2,1)S(1)}, u32[]{:S(2)}, u32[]{:S(2)}) async-start(bf16[224,64,12]{0,2,1:T(8,128)(2,1)} %reshape.95), calls=%async_computation.2 | async-start | bytes 1048576 | tf_op jit(solution)/shard_map/all_to_all | solution.py:53
Sparse Core Ops, SparseCore 0:
  110.6 74.5 all-gather.2
  190.8 85.2 all-gather.4
where the time goes:
time: 381 us
  waiting for transfers between devices  195 us (51%)
  blocking collectives  124 us (33%)
  starting transfers between devices  23.6 us (6%)
  between operations  13.6 us (4%)
  local copies, waits for them, and re-layouts  13.4 us (4%)
  matrix products  6.8 us (2%)
  other arithmetic  5.02 us (1%)
    all_to_all x1, blocking collectives, on_device(): lax.all_to_all(outgoing, 'tp', split_axis=0, concat_axis=0, tiled=True)  94.9 us
    all_gather x1, waiting for transfers between devices, on_device(): lax.all_gather(grad_up, 'ep', axis=0, tiled=True)  85.4 us
    all_to_all x1, waiting for transfers between devices, on_device(): lax.all_to_all(expert_grad.reshape(width_local, expert_count, capacity),...  65.2 us
    all_gather x1, waiting for transfers between devices, on_device(): segment = lax.all_gather(received, 'ep', axis=1, tiled=True)  44.3 us
    all_to_all x1, blocking collectives, on_device(): lax.all_to_all(down_local, 'ep', split_axis=0, concat_axis=1, tiled=True)  28.7 us
    all_to_all x1, starting transfers between devices, on_device(): lax.all_to_all(expert_grad.reshape(width_local, expert_count, capacity),...  23.5 us
  transfers between devices with their start and end apart: 3, of which 3 were waited for; matrix products, arithmetic and copies ran while one was open for 1% of the time, Pallas kernels for 0%

commit v1 on v0

v1 whole, which is shorter than its diff:
```python
import functools
import jax
import jax.numpy as jnp
from jax import lax
from jax.experimental import pallas as pl
from jax.experimental.pallas import tpu as pltpu
from jax.sharding import PartitionSpec as P

MESH = pl.DeviceIdType.MESH
F32 = jnp.float32
BF16 = jnp.bfloat16

CHIPS = 32
AWAY = [(-(p // 2) if p % 2 == 0 else (p + 1) // 2) % CHIPS for p in range(CHIPS)]
PLACE = [AWAY.index(r) for r in range(CHIPS)]
BACK = [PLACE[-r % CHIPS] for r in AWAY]
OWN = PLACE[0]
CAP = 12
PAIR = 2 * CAP
SLOTS = CHIPS * PAIR
TOK = 256
WIDTH = 224
LANES = 256
HID = 152
HALF = 80
CHUNKS = 6
CHUNK = SLOTS // CHUNKS
READY = [0, 6, 12, 18, 24, 30]
PARTS = (0, 384, 512, 768)


def nt_dot(a, b):
    return lax.dot_general(a, b, (((1,), (1,)), ((), ())), preferred_element_type=F32)


def to_message(rows):
    n = rows.shape[0] // PAIR
    blocks = rows.reshape(n, PAIR, LANES)
    return jnp.concatenate([blocks[:, :, :128], blocks[:, :, 128:]], axis=1).astype(BF16)


def from_message(message):
    wide = message.astype(F32)
    rows = jnp.concatenate([wide[:, :PAIR], wide[:, PAIR:]], axis=2)
    return rows.reshape(rows.shape[0] * PAIR, LANES)


def look_up(table, index):
    found = jnp.zeros_like(index)
    for i, value in enumerate(table):
        found = jnp.where(index == i, value, found)
    return found


def whole(k):
    return -(-k * CHUNK // PAIR)


def done(k):
    return k * CHUNK // PAIR


def kernel(
    grad_ref, route_ref, prob_ref, down_hbm, up_hbm, saved_hbm, out_ref,
    grads, routes, probs, down_in, up, saved, down,
    send, got, back, came, x32, y32, part, in_a, in_b, in_c, run, in_a2, in_b2, in_c2, gath, gu, eg,
    factor, picks, cols, mine, theirs,
    ls, zs, zr, rs, rr, xs, xr, fs, fr,
):
    ep = lax.axis_index("ep")
    me = lax.axis_index("tp")
    z = lax.div(me, 2)
    c = lax.rem(me, 2)
    x = lax.div(ep, 4)
    y = lax.rem(ep, 4)
    s = 1 - 2 * c
    sibling = (ep, 2 * z + 1 - c)

    def chip(r):
        return (ep, lax.rem(z + r, CHIPS) * 2 + c)

    def near(o, phase, coord):
        along_x = (o == 0) == (phase == 0)
        return (coord * 4 + y if along_x else x * 4 + coord, me)

    def ring(coord):
        return lax.rem(coord + s + 4, 4), lax.rem(coord - s + 4, 4), lax.rem(coord + 2, 4)

    barrier = pltpu.get_barrier_semaphore()

    def greet(r, carry):
        pl.semaphore_signal(barrier, inc=1, device_id=chip(r), device_id_type=MESH)
        return carry

    lax.fori_loop(1, CHIPS, greet, 0)
    pl.semaphore_signal(barrier, inc=1, device_id=sibling, device_id_type=MESH)
    for o in range(2):
        for step in (1, 2, 3):
            peer = near(o, 0, lax.rem((x if o == 0 else y) + step, 4))
            pl.semaphore_signal(barrier, inc=1, device_id=peer, device_id_type=MESH)
    loads = [
        pltpu.make_async_copy(src, dst, ls.at[i])
        for i, (src, dst) in enumerate([(down_hbm, down_in), (saved_hbm, saved), (up_hbm, up)])
    ]
    for load in loads:
        load.start()
    pl.semaphore_wait(barrier, CHIPS - 1 + 1 + 6)

    trades = [
        pltpu.make_async_remote_copy(
            src_ref=src, dst_ref=dst.at[c], send_sem=fs.at[i], recv_sem=fr.at[i],
            device_id=sibling, device_id_type=MESH,
        )
        for i, (src, dst) in enumerate([(route_ref, routes), (prob_ref, probs), (grad_ref, grads)])
    ]
    for trade in trades:
        trade.start()
    grads[c] = grad_ref[...]
    routes[c] = route_ref[...]
    probs[c] = prob_ref[...]

    expert = lax.broadcasted_iota(jnp.int32, (64, 1), 0)
    away = ((expert >> 1) - z + CHIPS) & (CHIPS - 1)
    place_to = look_up(PLACE, away)
    place_from = look_up(BACK, place_to)
    base_to = jnp.where((expert & 1) == c, place_to * PAIR, -4096).astype(F32)
    base_from = jnp.where((expert & 1) == c, place_from * PAIR, -4096).astype(F32)
    experts = lax.broadcasted_iota(jnp.int32, (64, TOK), 0)
    earlier = jnp.where(
        lax.broadcasted_iota(jnp.int32, (TOK, TOK), 0) < lax.broadcasted_iota(jnp.int32, (TOK, TOK), 1),
        1.0, 0.0,
    ).astype(BF16)
    rows = lax.broadcasted_iota(jnp.int32, (SLOTS, TOK), 0).astype(F32)

    def tokens_of(block):
        route = routes[block]
        first = jnp.where(experts == route[0:1], 1.0, 0.0)
        second = jnp.where(experts == route[1:2], 1.0, 0.0)
        before = jnp.dot((first + second).astype(BF16), earlier, preferred_element_type=F32)
        shift = (CAP * block).astype(F32)
        one, two, one_from, two_from = [
            jnp.sum(hot * (before + base), axis=0, keepdims=True) + shift
            for base in (base_to, base_from)
            for hot in (first, second)
        ]
        hot = jnp.where((rows == one) | (rows == two), 1.0, 0.0).astype(BF16)
        wide = jnp.concatenate([grads[block], jnp.zeros((LANES - WIDTH, TOK), BF16)], axis=0)
        return nt_dot(hot, wide), [one_from, two_from, probs[block]]

    total, found = tokens_of(c)
    for trade in trades:
        trade.wait_recv()
    other, other_found = tokens_of(1 - c)
    send[...] = to_message(total + other)

    def dispatch(p, group):
        i = BACK[p]
        return pltpu.make_async_remote_copy(
            src_ref=send.at[i], dst_ref=got.at[p], send_sem=zs, recv_sem=zr.at[group],
            device_id=chip(AWAY[i]), device_id_type=MESH,
        )

    def send_back(p, group):
        return pltpu.make_async_remote_copy(
            src_ref=back.at[p], dst_ref=came.at[p], send_sem=rs, recv_sem=rr.at[group],
            device_id=chip(AWAY[p]), device_id_type=MESH,
        )

    def each_place(lo, hi, act):
        for p in range(lo, hi):
            if p != OWN:
                act(p)

    def group_ref(buffer, lo, hi):
        return buffer.at[lo:hi - (1 if lo <= OWN < hi else 0)]

    def group_arrived(buffer, lo, hi, sem):
        ref = group_ref(buffer, lo, hi)
        pltpu.make_async_remote_copy(
            src_ref=ref, dst_ref=ref, send_sem=zs, recv_sem=sem, device_id=sibling, device_id_type=MESH,
        ).wait_recv()

    def group_left(buffer, sem):
        ref = group_ref(buffer, 0, CHIPS)
        pltpu.make_async_remote_copy(
            src_ref=ref, dst_ref=ref, send_sem=sem, recv_sem=zr.at[0], device_id=sibling, device_id_type=MESH,
        ).wait_send()

    for k in range(CHUNKS):
        each_place(whole(k), whole(k + 1), lambda p, k=k: dispatch(p, k).start())
    got[OWN] = send[OWN]

    loads[0].wait()

    def turn(j, carry):
        at = pl.multiple_of(128 * j, 128)
        block = down_in[:, pl.ds(at, 128)].astype(F32)
        block = jnp.concatenate([block, jnp.zeros((LANES - WIDTH, 128), F32)], axis=0)
        down[pl.ds(at, 128), :] = block.T.astype(BF16)
        return carry

    lax.fori_loop(0, 16 * HID // 128, turn, 0)
    loads[1].wait()
    lane = lax.broadcasted_iota(jnp.int32, (1, SLOTS), 1)
    place = (lane * 2731) >> 16
    source = ((z + look_up(AWAY, place)) & (CHIPS - 1)) * PAIR + (lane - PAIR * place)
    order = jnp.where(
        lax.broadcasted_iota(jnp.int32, (SLOTS, SLOTS), 0) == source, 1.0, 0.0
    ).astype(BF16)
    u = jnp.dot(saved[...], order, preferred_element_type=F32)
    g = 1.0 / (1.0 + jnp.exp(-u))
    factor[0:HID] = g * (1.0 + u * (1.0 - g))
    factor[HID:] = jnp.zeros((2 * HALF - HID, SLOTS), F32)
    cols[...] = jnp.concatenate(found + other_found + [jnp.zeros((120, TOK), F32)], axis=0).T
    lanes = lax.broadcasted_iota(jnp.int32, (TOK, SLOTS), 1).astype(F32)
    for i, column in enumerate((0, 1, 4, 5)):
        picks[i] = jnp.where(lanes == cols[:, column:column + 1], 1.0, 0.0).astype(BF16)
    loads[2].wait()

    def transfers(k, o):
        a, b = (x, y) if o == 0 else (y, x)
        ap, am, a2 = ring(a)
        bp, bm, b2 = ring(b)
        ga = gath.at[k, o]
        return [
            (part.at[k, o, a2], in_a.at[k, o], near(o, 0, ap), in_a.at[k, o]),
            (part.at[k, o, am], in_b.at[k, o], near(o, 0, am), in_b.at[k, o]),
            (part.at[k, o, ap], in_c.at[k, o], near(o, 0, ap), in_c.at[k, o]),
            (run.at[k, o, bp], in_a2.at[k, o], near(o, 1, bp), in_a2.at[k, o]),
            (run.at[k, o, bm], in_b2.at[k, o], near(o, 1, bm), in_b2.at[k, o]),
            (run.at[k, o, b2], in_c2.at[k, o], near(o, 1, b2), in_c2.at[k, o]),
            (ga.at[a, b], ga.at[a, b], near(o, 1, bp), ga.at[a, bm]),
            (ga.at[a, b], ga.at[a, b], near(o, 1, bm), ga.at[a, bp]),
            (ga.at[a, b], ga.at[a, b], near(o, 1, b2), ga.at[a, b2]),
            (ga.at[a], ga.at[a], near(o, 0, ap), ga.at[am]),
            (ga.at[a], ga.at[a], near(o, 0, am), ga.at[ap]),
            (ga.at[am], ga.at[am], near(o, 0, ap), ga.at[a2]),
        ]

    def link(k, o, q, src, dst, peer):
        return pltpu.make_async_remote_copy(
            src_ref=src, dst_ref=dst, send_sem=xs.at[k, o, q], recv_sem=xr.at[k, o, q],
            device_id=peer, device_id_type=MESH,
        )

    def start(k, o, *qs):
        for q in qs:
            src, dst, peer, _ = transfers(k, o)[q]
            link(k, o, q, src, dst, peer).start()

    def arrived(k, o, *qs):
        for q in qs:
            _, _, peer, land = transfers(k, o)[q]
            link(k, o, q, land, land, peer).wait_recv()

    def left(k, o, *qs):
        for q in qs:
            src, dst, peer, _ = transfers(k, o)[q]
            link(k, o, q, src, dst, peer).wait_send()

    def stage0(k):
        lo, hi = whole(k), whole(k + 1)
        group_arrived(got, lo, hi, zr.at[k])
        x32[PAIR * lo:PAIR * hi] = from_message(got[lo:hi])
        tokens = x32[k * CHUNK:(k + 1) * CHUNK].astype(BF16)

        def pair(i, carry):
            weights = down[pl.ds(pl.multiple_of(2 * HID * i, 16), 2 * HID), :]
            hidden = nt_dot(weights, tokens)
            px = lax.div(i, 2)
            for j in range(2):
                py = 2 * lax.rem(i, 2) + j
                block = hidden[j * HID:(j + 1) * HID]
                part[k, 0, px, py] = block[0:HALF].astype(BF16)
                part[k, 1, py, px] = jnp.concatenate(
                    [block[HALF:], jnp.zeros((2 * HALF - HID, CHUNK), F32)], axis=0
                ).astype(BF16)
            return carry

        lax.fori_loop(0, 8, pair, 0)
        for o in range(2):
            start(k, o, 0, 1)

    def stage1(k):
        for o in range(2):
            ap, _, _ = ring(x if o == 0 else y)
            arrived(k, o, 0)
            part[k, o, ap] = (part[k, o, ap].astype(F32) + in_a[k, o].astype(F32)).astype(BF16)
            start(k, o, 2)

    def stage2(k):
        for o in range(2):
            arrived(k, o, 1, 2)
            a = x if o == 0 else y
            run[k, o] = (
                part[k, o, a].astype(F32) + in_b[k, o].astype(F32) + in_c[k, o].astype(F32)
            ).astype(BF16)
            start(k, o, 3, 4, 5)

    def stage3(k):
        for o in range(2):
            arrived(k, o, 3, 4, 5)
            a, b = (x, y) if o == 0 else (y, x)
            hidden = run[k, o, b].astype(F32) + in_a2[k, o].astype(F32)
            hidden = hidden + in_b2[k, o].astype(F32) + in_c2[k, o].astype(F32)
            slope = factor[o * HALF:(o + 1) * HALF, k * CHUNK:(k + 1) * CHUNK]
            gath[k, o, a, b] = (hidden * slope).astype(BF16)
            start(k, o, 6, 7, 8)

    def stage4(k):
        for o in range(2):
            arrived(k, o, 6, 7, 8)
            start(k, o, 9, 10)

    def stage5(k):
        for o in range(2):
            arrived(k, o, 9)
            start(k, o, 11)

    def stage6(k):
        for o in range(2):
            arrived(k, o, 10, 11)

        def pair(i, carry):
            px = lax.div(i, 2)
            pieces = []
            for j in range(2):
                py = 2 * lax.rem(i, 2) + j
                pieces.append(gath[k, 0, px, py].astype(F32))
                pieces.append(gath[k, 1, py, px].astype(F32)[0:HID - HALF])
            gu[pl.ds(pl.multiple_of(2 * HID * i, 16), 2 * HID), :] = jnp.concatenate(pieces, axis=0).astype(BF16)
            return carry

        lax.fori_loop(0, 8, pair, 0)
        result = jnp.dot(up[...], gu[...], preferred_element_type=F32)
        padded = jnp.concatenate([result, jnp.zeros((LANES - WIDTH, CHUNK), F32)], axis=0)
        eg[k * CHUNK:(k + 1) * CHUNK] = padded.T
        lo, hi = done(k), done(k + 1)
        back[lo:hi] = to_message(eg[PAIR * lo:PAIR * hi])
        each_place(lo, hi, lambda p: send_back(p, k).start())
        if lo <= OWN < hi:
            came[OWN] = back[OWN]
        for o in range(2):
            left(k, o, *range(12))

    stages = [stage0, stage1, stage2, stage3, stage4, stage5, stage6]
    offsets = [0, 4, 7, 10.5, 13.5, 17.5, 20.5]
    plan = sorted((READY[k] + offsets[i], k, i) for k in range(CHUNKS) for i in range(len(stages)))
    for _, k, i in plan:
        stages[i](k)
    group_left(send, zs)
    for trade in trades:
        trade.wait_send()

    sums = [None, None]
    taken = 0
    for lo, hi in zip(PARTS[:-1], PARTS[1:]):
        while done(taken) * PAIR < hi:
            first, last = done(taken), done(taken + 1)
            group_arrived(came, first, last, rr.at[taken])
            y32[PAIR * first:PAIR * last] = from_message(came[first:last])
            taken += 1
        slots = y32[lo:hi].astype(BF16)
        for i in range(2):
            for k in range(2):
                term = jnp.dot(picks[2 * i + k, :, lo:hi], slots, preferred_element_type=F32)
                term = term * cols[:, 4 * i + 2 + k:4 * i + 3 + k]
                sums[i] = term if sums[i] is None else sums[i] + term
    mine[...] = sums[1]
    swap = pltpu.make_async_remote_copy(
        src_ref=mine, dst_ref=theirs, send_sem=fs.at[3], recv_sem=fr.at[3],
        device_id=sibling, device_id_type=MESH,
    )
    swap.start()
    group_left(back, rs)
    swap.wait_recv()
    out_ref[...] = (sums[0] + theirs[...]).T[0:WIDTH].astype(BF16)
    swap.wait_send()


def on_device(grad_out, route_probs, routes, saved_up, w_up, w_down):
    vmem = pl.BlockSpec(memory_space=pltpu.VMEM)
    hbm = pl.BlockSpec(memory_space=pl.ANY)
    dma = pltpu.SemaphoreType.DMA
    message = pltpu.VMEM((CHIPS, 2 * PAIR, 128), BF16)
    slot_rows = pltpu.VMEM((SLOTS, LANES), F32)
    blocks = pltpu.VMEM((CHUNKS, 2, 4, 4, HALF, CHUNK), BF16)
    line = pltpu.VMEM((CHUNKS, 2, 4, HALF, CHUNK), BF16)
    block = pltpu.VMEM((CHUNKS, 2, HALF, CHUNK), BF16)
    flops = 2 * 2 * SLOTS * 16 * HID * WIDTH
    result = pl.pallas_call(
        kernel,
        name="experts",
        out_shape=jax.ShapeDtypeStruct((WIDTH, TOK), BF16),
        in_specs=[vmem, vmem, vmem, hbm, hbm, hbm],
        out_specs=vmem,
        scratch_shapes=[
            pltpu.VMEM((2, WIDTH, TOK), BF16),
            pltpu.VMEM((2, 2, TOK), jnp.int32),
            pltpu.VMEM((2, 2, TOK), F32),
            pltpu.VMEM((WIDTH, 16 * HID), BF16),
            pltpu.VMEM((WIDTH, 16 * HID), BF16),
            pltpu.VMEM((HID, SLOTS), BF16),
            pltpu.VMEM((16 * HID, LANES), BF16),
            message,
            message,
            message,
            message,
            slot_rows,
            slot_rows,
            blocks,
            line,
            line,
            line,
            line,
            block,
            block,
            block,
            blocks,
            pltpu.VMEM((16 * HID, CHUNK), BF16),
            slot_rows,
            pltpu.VMEM((2 * HALF, SLOTS), F32),
            pltpu.VMEM((4, TOK, SLOTS), BF16),
            pltpu.VMEM((TOK, 128), F32),
            pltpu.VMEM((TOK, LANES), F32),
            pltpu.VMEM((TOK, LANES), F32),
            dma((3,)),
            dma,
            dma((CHUNKS,)),
            dma,
            dma((CHUNKS,)),
            dma((CHUNKS, 2, 12)),
            dma((CHUNKS, 2, 12)),
            dma((4,)),
            dma((4,)),
        ],
        compiler_params=pltpu.CompilerParams(
            collective_id=0, has_side_effects=True, vmem_limit_bytes=56 * 2**20
        ),
        cost_estimate=pl.CostEstimate(flops=flops, bytes_accessed=3 * 2**20, transcendentals=0),
    )(grad_out.T, routes.T, route_probs.T, w_down[0].T, w_up[0], saved_up[0])
    return result.T


def solution(mesh):
    return jax.shard_map(
        on_device,
        mesh=mesh,
        in_specs=(
            P("tp", "ep"),
            P("tp", None),
            P("tp", None),
            P("tp", "ep", None),
            P("tp", "ep", None),
            P("tp", None, "ep"),
        ),
        out_specs=P("tp", "ep"),
        check_vma=False,
    )
```

time: 381 us -> 127 us (0.33)
  the two profiles are of different devices: /device:TPU:2 before, /device:TPU:41 now
where the time goes in v1:
time: 127 us
  Pallas kernels  125 us (98%)
  local copies, waits for them, and re-layouts  1.55 us (1%)
    pallas_call x1, Pallas kernels, on_device(): pl.pallas_call(kernel, name='experts', out_shape=jax.ShapeDtypeStruct((WI...  125 us

profile of v1, /device:TPU:41, one launch (start us, length us, event | category | flops | bytes accessed | tf_op | source)
XLA Modules:
  0.0 126.6 jit_solution(2683258656562619160)
XLA Ops:
  0.0 125.0 %experts.1 = bf16[224,256]{1,0:T(8,128)(2,1)} custom-call(bf16[224,256]{1,0:T(8,128)(2,1)} %bitcast.13, s32[2,256]{1,0:T(2,128)} %bitcast.14, f32[2,256]{1,0:T(2,128)} %bitcast.15, bf16[224,2432]{1,0:T(8,128)(2,1)} %bitcast.10, bf16[224,2432]{1,0:T(8,128)(2,1)} %bitcast.11, bf16[152,768]{1,0:T(8,128)(2,1)} %bitcast.12), custom_call_target="tpu_custom_call" | custom-call | flops 1673527296 | bytes 3145728 | tf_op jit(solution)/shard_map/experts/pallas_call | solution.py:391
  125.0 1.6 %copy.8 = bf16[256,224]{0,1:T(8,128)(2,1)} copy(bf16[256,224]{0,1:T(8,128)(2,1)} %bitcast.9) | data formatting | bytes 229376

commit v2 on v1

--- a/solution.py
+++ b/solution.py
@@ -200,22 +200,24 @@
         return carry
 
     lax.fori_loop(0, 16 * HID // 128, turn, 0)
-    loads[1].wait()
-    lane = lax.broadcasted_iota(jnp.int32, (1, SLOTS), 1)
-    place = (lane * 2731) >> 16
-    source = ((z + look_up(AWAY, place)) & (CHIPS - 1)) * PAIR + (lane - PAIR * place)
-    order = jnp.where(
-        lax.broadcasted_iota(jnp.int32, (SLOTS, SLOTS), 0) == source, 1.0, 0.0
-    ).astype(BF16)
-    u = jnp.dot(saved[...], order, preferred_element_type=F32)
-    g = 1.0 / (1.0 + jnp.exp(-u))
-    factor[0:HID] = g * (1.0 + u * (1.0 - g))
-    factor[HID:] = jnp.zeros((2 * HALF - HID, SLOTS), F32)
-    cols[...] = jnp.concatenate(found + other_found + [jnp.zeros((120, TOK), F32)], axis=0).T
-    lanes = lax.broadcasted_iota(jnp.int32, (TOK, SLOTS), 1).astype(F32)
-    for i, column in enumerate((0, 1, 4, 5)):
-        picks[i] = jnp.where(lanes == cols[:, column:column + 1], 1.0, 0.0).astype(BF16)
-    loads[2].wait()
+    def make_factor():
+        loads[1].wait()
+        lane = lax.broadcasted_iota(jnp.int32, (1, SLOTS), 1)
+        place = (lane * 2731) >> 16
+        source = ((z + look_up(AWAY, place)) & (CHIPS - 1)) * PAIR + (lane - PAIR * place)
+        order = jnp.where(
+            lax.broadcasted_iota(jnp.int32, (SLOTS, SLOTS), 0) == source, 1.0, 0.0
+        ).astype(BF16)
+        u = jnp.dot(saved[...], order, preferred_element_type=F32)
+        g = 1.0 / (1.0 + jnp.exp(-u))
+        factor[0:HID] = g * (1.0 + u * (1.0 - g))
+        factor[HID:] = jnp.zeros((2 * HALF - HID, SLOTS), F32)
+
+    def make_picks():
+        cols[...] = jnp.concatenate(found + other_found + [jnp.zeros((120, TOK), F32)], axis=0).T
+        lanes = lax.broadcasted_iota(jnp.int32, (TOK, SLOTS), 1).astype(F32)
+        for i, column in enumerate((0, 1, 4, 5)):
+            picks[i] = jnp.where(lanes == cols[:, column:column + 1], 1.0, 0.0).astype(BF16)
 
     def transfers(k, o):
         a, b = (x, y) if o == 0 else (y, x)
@@ -340,15 +342,21 @@
         each_place(lo, hi, lambda p: send_back(p, k).start())
         if lo <= OWN < hi:
             came[OWN] = back[OWN]
-        for o in range(2):
-            left(k, o, *range(12))
 
     stages = [stage0, stage1, stage2, stage3, stage4, stage5, stage6]
     offsets = [0, 4, 7, 10.5, 13.5, 17.5, 20.5]
     plan = sorted((READY[k] + offsets[i], k, i) for k in range(CHUNKS) for i in range(len(stages)))
     for _, k, i in plan:
         stages[i](k)
+        if (k, i) == (0, 0):
+            make_factor()
+        if (k, i) == (0, 1):
+            make_picks()
+            loads[2].wait()
     group_left(send, zs)
+    for k in range(CHUNKS):
+        for o in range(2):
+            left(k, o, *range(12))
     for trade in trades:
         trade.wait_send()
 

time: 127 us -> 127 us (level)
  no operation moved by 1% of the time
where the time goes in v2:
time: 127 us; the launch traced here: 126 us
  Pallas kernels  125 us (98%)
  local copies, waits for them, and re-layouts  1.55 us (1%)
    pallas_call x1, Pallas kernels, on_device(): pl.pallas_call(kernel, name='experts', out_shape=jax.ShapeDtypeStruct((WI...  125 us

profile of v2, /device:TPU:41, one launch (start us, length us, event | category | flops | bytes accessed | tf_op | source)
XLA Modules:
  0.0 126.2 jit_solution(5741523944773202537)
XLA Ops:
  0.0 124.7 %experts.1 = bf16[224,256]{1,0:T(8,128)(2,1)} custom-call(bf16[224,256]{1,0:T(8,128)(2,1)} %bitcast.13, s32[2,256]{1,0:T(2,128)} %bitcast.14, f32[2,256]{1,0:T(2,128)} %bitcast.15, bf16[224,2432]{1,0:T(8,128)(2,1)} %bitcast.10, bf16[224,2432]{1,0:T(8,128)(2,1)} %bitcast.11, bf16[152,768]{1,0:T(8,128)(2,1)} %bitcast.12), custom_call_target="tpu_custom_call" | custom-call | flops 1673527296 | bytes 3145728 | tf_op jit(solution)/shard_map/experts/pallas_call | solution.py:399
  124.7 1.6 %copy.8 = bf16[256,224]{0,1:T(8,128)(2,1)} copy(bf16[256,224]{0,1:T(8,128)(2,1)} %bitcast.9) | data formatting | bytes 229376
